TPU v7x, 256 devices: a whole 4x4x8 slice. The times are simulated.
256 devices in a mesh: row: 16 (over y, z_lo, core), col: 16 (over x, z_hi).
Axes of the slice: x: 4, y: 4, z: 8 (z_hi: 4, z_lo: 2; z = z_hi * 2 + z_lo), core: 2. Of those that a mesh axis runs over, the one named last changes fastest.
Arguments:
- points: float32 [16, 65536], P(None, ('row', 'col')), may hold values from -6 to 6
- inv_length: float32 [16], replicated, may hold values from 0.2 to 0.6
- solution: float32 [16, 65536], P(None, ('row', 'col')), may hold values from -6 to 6
- residual: float32 [16, 65536], P(None, ('row', 'col')), may hold values from -6 to 6
- direction: float32 [16, 65536], P(None, ('row', 'col')), may hold values from -6 to 6
Outputs:
- new_solution: float32 [16, 65536], P(None, ('row', 'col'))
- new_residual: float32 [16, 65536], P(None, ('row', 'col'))
- new_direction: float32 [16, 65536], P(None, ('row', 'col'))
All inputs are finite; a program needn't handle non-finite values.
Results may differ from a plain program's by a relative error of at most 0.00013.
Values sent between devices are 32-bit elements; how exact they have to be, the bound alone decides.
A program may use at most 64 MiB of HBM per device.

v0:
```python
import math

import jax
import jax.numpy as jnp
from jax import lax
from jax.sharding import PartitionSpec as P


def kernel_tile_of(query, query_sq, key_scaled, key_sq):
    inner_prod = jnp.einsum("fi,fj->ij", query, key_scaled, precision=lax.Precision.HIGHEST)
    dist = jnp.maximum(query_sq[:, None] + key_sq[None, :] - 2.0 * inner_prod, 0.0)
    return jnp.exp(-0.5 * dist)


def split_blocks(scaled):
    point_count = scaled.shape[1]
    block_width = math.gcd(point_count, 512)
    nblocks = point_count // block_width
    squares = jnp.sum(scaled * scaled, axis=0)
    query_blocks = scaled.reshape(scaled.shape[0], nblocks, block_width).transpose(1, 0, 2)
    return (query_blocks, squares.reshape(nblocks, block_width))


def on_device(points, inv_length, solution, residual, direction):
    factor = inv_length[:, None]
    probes = direction.shape[0]
    old_norm = lax.psum(jnp.sum(residual * residual, axis=1), ("row", "col"))
    gathered = lax.all_gather(points, "col", axis=1, tiled=True)
    query_blocks, query_squares = split_blocks(gathered * factor)
    key_points = lax.all_gather(points, "row", axis=1, tiled=True)
    key_vecs = lax.all_gather(direction, "row", axis=1, tiled=True)
    key_scaled = key_points * factor
    key_sq = jnp.sum(key_scaled * key_scaled, axis=0)

    def one_block(block_args):
        query, query_sq = block_args
        kernel_tile = kernel_tile_of(query, query_sq, key_scaled, key_sq)
        return jnp.einsum("ij,pj->pi", kernel_tile, key_vecs, precision=lax.Precision.HIGHEST)

    partial_terms = lax.map(one_block, (query_blocks, query_squares))
    row_terms = partial_terms.transpose(1, 0, 2).reshape(probes, -1)
    kernel_image = lax.psum_scatter(row_terms, "col", scatter_dimension=1, tiled=True)
    curvature = lax.psum(jnp.sum(direction * kernel_image, axis=1), ("row", "col"))
    step_size = old_norm / curvature
    new_residual = residual - step_size[:, None] * kernel_image
    new_norm = lax.psum(jnp.sum(new_residual * new_residual, axis=1), ("row", "col"))
    new_solution = solution + step_size[:, None] * direction
    new_direction = new_residual + (new_norm / old_norm)[:, None] * direction
    return (new_solution, new_residual, new_direction)


def solution(mesh):
    return jax.shard_map(
        on_device,
        mesh=mesh,
        in_specs=(
            P(None, ("row", "col")),
            P(),
            P(None, ("row", "col")),
            P(None, ("row", "col")),
            P(None, ("row", "col")),
        ),
        out_specs=(P(None, ("row", "col")), P(None, ("row", "col")), P(None, ("row", "col"))),
        check_vma=False,
    )
```

profile of v0, /device:TPU:1, one launch (start us, length us, event | category | flops | bytes accessed | tf_op | source)
XLA Modules:
  0.0 456.2 jit_solution(11103734644619097421)
XLA Ops:
  7.2 0.0 reduce-scatter.2.cloned.1.call-start
  7.2 22.9 %all_gather.10 = f32[16,4096]{1,0:T(8,128)S(1)} all-gather(f32[16,256]{1,0:T(8,128)} %param.7), channel_id=1, replica_groups=mesh['row'=16,'col'=16] {'row'}, dimensions={1}, use_global_device_ids=true | all-gather | bytes 278528 | tf_op jit(solution)/shard_map/all_gather | solution.py:30
  30.1 40.2 %all_gather.9 = f32[16,4096]{1,0:T(8,128)S(1)} all-gather(f32[16,256]{1,0:T(8,128)} %param.7), channel_id=1, replica_groups=mesh['row'=16,'col'=16] {'col'}, dimensions={1}, use_global_device_ids=true | all-gather | bytes 278528 | tf_op jit(solution)/shard_map/all_gather | solution.py:28
  70.3 0.8 multiply_reduce_fusion
  71.2 24.4 %all_gather.11 = f32[16,4096]{1,0:T(8,128)S(1)} all-gather(f32[16,256]{1,0:T(8,128)} %param.11), channel_id=1, replica_groups=mesh['row'=16,'col'=16] {'row'}, dimensions={1}, use_global_device_ids=true | all-gather | bytes 278528 | tf_op jit(solution)/shard_map/all_gather | solution.py:31
  95.6 125.8 %while.10 = (s32[]{:T(128)}, f32[8,16,512]{2,1,0:T(8,128)S(1)}, f32[8,512]{1,0:T(8,128)S(1)}, f32[4096]{0:T(1024)S(1)}, f32[8,16,512]{2,1,0:T(8,128)S(1)}, /*ind...) while((s32[]{:T(128)}, f32[8,16,512]{2,1,0:T(8,128)S(1)}, f32[8,512]{1,0:T(8,128)S(1)}, ...), condition=%wide.region_5.6_spmd, body=%wide.region_4.5_spmd.sunk | while | flops 815792128 | bytes 17389664 | solution.py:40
  95.6 6.7 %fusion.37 = f32[512,4096]{1,0:T(8,128)S(1)} fusion(f32[16,4096]{1,0:T(8,128)S(1)} %get-tuple-element.131, f32[8,16,512]{2,1,0:T(8,128)S(1)} %get-tuple-element.130, s32[]{:T(128)} %get-tuple-element.118), kind=kOutput, calls=%fused_computation.14.clone.1 | convolution fusion | flops 402653184 | bytes 8683524 | tf_op jit(solution)/shard_map/while/body/eval_jaxpr/fi,fj->ij/dot_general | solution.py:10
  102.3 9.0 %fusion.38 = f32[8,16,512]{2,1,0:T(8,128)S(1)} fusion(f32[8,16,512]{2,1,0:T(8,128)S(1)} %get-tuple-element.119, s32[]{:T(128)} %get-tuple-element.118, f32[16,4096]{1,0:T(8,128)S(1)} %get-tuple-element.132, f32[512,4096]{1,0:T(8,128)S(1)} %fusion.37, f32[4096]{0:T(1024)S(1)} %get-tuple-element.129, f32[512]{0:T(512)S(1)} %bitcast.36), kind=kOutput, calls=%fused_computation.13.clone.1 | convolution fusion | flops 413138944 | bytes 8701956 | tf_op jit(solution)/shard_map/while/body/eval_jaxpr/ij,pj->pi/dot_general | solution.py:38
  111.3 6.7 %fusion.37 = f32[512,4096]{1,0:T(8,128)S(1)} fusion(f32[16,4096]{1,0:T(8,128)S(1)} %get-tuple-element.131, f32[8,16,512]{2,1,0:T(8,128)S(1)} %get-tuple-element.130, s32[]{:T(128)} %get-tuple-element.118), kind=kOutput, calls=%fused_computation.14.clone.1 | convolution fusion | flops 402653184 | bytes 8683524 | tf_op jit(solution)/shard_map/while/body/eval_jaxpr/fi,fj->ij/dot_general | solution.py:10
  118.1 9.0 %fusion.38 = f32[8,16,512]{2,1,0:T(8,128)S(1)} fusion(f32[8,16,512]{2,1,0:T(8,128)S(1)} %get-tuple-element.119, s32[]{:T(128)} %get-tuple-element.118, f32[16,4096]{1,0:T(8,128)S(1)} %get-tuple-element.132, f32[512,4096]{1,0:T(8,128)S(1)} %fusion.37, f32[4096]{0:T(1024)S(1)} %get-tuple-element.129, f32[512]{0:T(512)S(1)} %bitcast.36), kind=kOutput, calls=%fused_computation.13.clone.1 | convolution fusion | flops 413138944 | bytes 8701956 | tf_op jit(solution)/shard_map/while/body/eval_jaxpr/ij,pj->pi/dot_general | solution.py:38
  127.0 6.7 %fusion.37 = f32[512,4096]{1,0:T(8,128)S(1)} fusion(f32[16,4096]{1,0:T(8,128)S(1)} %get-tuple-element.131, f32[8,16,512]{2,1,0:T(8,128)S(1)} %get-tuple-element.130, s32[]{:T(128)} %get-tuple-element.118), kind=kOutput, calls=%fused_computation.14.clone.1 | convolution fusion | flops 402653184 | bytes 8683524 | tf_op jit(solution)/shard_map/while/body/eval_jaxpr/fi,fj->ij/dot_general | solution.py:10
  133.8 9.0 %fusion.38 = f32[8,16,512]{2,1,0:T(8,128)S(1)} fusion(f32[8,16,512]{2,1,0:T(8,128)S(1)} %get-tuple-element.119, s32[]{:T(128)} %get-tuple-element.118, f32[16,4096]{1,0:T(8,128)S(1)} %get-tuple-element.132, f32[512,4096]{1,0:T(8,128)S(1)} %fusion.37, f32[4096]{0:T(1024)S(1)} %get-tuple-element.129, f32[512]{0:T(512)S(1)} %bitcast.36), kind=kOutput, calls=%fused_computation.13.clone.1 | convolution fusion | flops 413138944 | bytes 8701956 | tf_op jit(solution)/shard_map/while/body/eval_jaxpr/ij,pj->pi/dot_general | solution.py:38
  142.8 6.7 %fusion.37 = f32[512,4096]{1,0:T(8,128)S(1)} fusion(f32[16,4096]{1,0:T(8,128)S(1)} %get-tuple-element.131, f32[8,16,512]{2,1,0:T(8,128)S(1)} %get-tuple-element.130, s32[]{:T(128)} %get-tuple-element.118), kind=kOutput, calls=%fused_computation.14.clone.1 | convolution fusion | flops 402653184 | bytes 8683524 | tf_op jit(solution)/shard_map/while/body/eval_jaxpr/fi,fj->ij/dot_general | solution.py:10
  149.5 9.0 %fusion.38 = f32[8,16,512]{2,1,0:T(8,128)S(1)} fusion(f32[8,16,512]{2,1,0:T(8,128)S(1)} %get-tuple-element.119, s32[]{:T(128)} %get-tuple-element.118, f32[16,4096]{1,0:T(8,128)S(1)} %get-tuple-element.132, f32[512,4096]{1,0:T(8,128)S(1)} %fusion.37, f32[4096]{0:T(1024)S(1)} %get-tuple-element.129, f32[512]{0:T(512)S(1)} %bitcast.36), kind=kOutput, calls=%fused_computation.13.clone.1 | convolution fusion | flops 413138944 | bytes 8701956 | tf_op jit(solution)/shard_map/while/body/eval_jaxpr/ij,pj->pi/dot_general | solution.py:38
  158.5 6.7 %fusion.37 = f32[512,4096]{1,0:T(8,128)S(1)} fusion(f32[16,4096]{1,0:T(8,128)S(1)} %get-tuple-element.131, f32[8,16,512]{2,1,0:T(8,128)S(1)} %get-tuple-element.130, s32[]{:T(128)} %get-tuple-element.118), kind=kOutput, calls=%fused_computation.14.clone.1 | convolution fusion | flops 402653184 | bytes 8683524 | tf_op jit(solution)/shard_map/while/body/eval_jaxpr/fi,fj->ij/dot_general | solution.py:10
  165.3 9.0 %fusion.38 = f32[8,16,512]{2,1,0:T(8,128)S(1)} fusion(f32[8,16,512]{2,1,0:T(8,128)S(1)} %get-tuple-element.119, s32[]{:T(128)} %get-tuple-element.118, f32[16,4096]{1,0:T(8,128)S(1)} %get-tuple-element.132, f32[512,4096]{1,0:T(8,128)S(1)} %fusion.37, f32[4096]{0:T(1024)S(1)} %get-tuple-element.129, f32[512]{0:T(512)S(1)} %bitcast.36), kind=kOutput, calls=%fused_computation.13.clone.1 | convolution fusion | flops 413138944 | bytes 8701956 | tf_op jit(solution)/shard_map/while/body/eval_jaxpr/ij,pj->pi/dot_general | solution.py:38
  174.2 6.7 %fusion.37 = f32[512,4096]{1,0:T(8,128)S(1)} fusion(f32[16,4096]{1,0:T(8,128)S(1)} %get-tuple-element.131, f32[8,16,512]{2,1,0:T(8,128)S(1)} %get-tuple-element.130, s32[]{:T(128)} %get-tuple-element.118), kind=kOutput, calls=%fused_computation.14.clone.1 | convolution fusion | flops 402653184 | bytes 8683524 | tf_op jit(solution)/shard_map/while/body/eval_jaxpr/fi,fj->ij/dot_general | solution.py:10
  181.0 9.0 %fusion.38 = f32[8,16,512]{2,1,0:T(8,128)S(1)} fusion(f32[8,16,512]{2,1,0:T(8,128)S(1)} %get-tuple-element.119, s32[]{:T(128)} %get-tuple-element.118, f32[16,4096]{1,0:T(8,128)S(1)} %get-tuple-element.132, f32[512,4096]{1,0:T(8,128)S(1)} %fusion.37, f32[4096]{0:T(1024)S(1)} %get-tuple-element.129, f32[512]{0:T(512)S(1)} %bitcast.36), kind=kOutput, calls=%fused_computation.13.clone.1 | convolution fusion | flops 413138944 | bytes 8701956 | tf_op jit(solution)/shard_map/while/body/eval_jaxpr/ij,pj->pi/dot_general | solution.py:38
  190.0 6.7 %fusion.37 = f32[512,4096]{1,0:T(8,128)S(1)} fusion(f32[16,4096]{1,0:T(8,128)S(1)} %get-tuple-element.131, f32[8,16,512]{2,1,0:T(8,128)S(1)} %get-tuple-element.130, s32[]{:T(128)} %get-tuple-element.118), kind=kOutput, calls=%fused_computation.14.clone.1 | convolution fusion | flops 402653184 | bytes 8683524 | tf_op jit(solution)/shard_map/while/body/eval_jaxpr/fi,fj->ij/dot_general | solution.py:10
  196.7 9.0 %fusion.38 = f32[8,16,512]{2,1,0:T(8,128)S(1)} fusion(f32[8,16,512]{2,1,0:T(8,128)S(1)} %get-tuple-element.119, s32[]{:T(128)} %get-tuple-element.118, f32[16,4096]{1,0:T(8,128)S(1)} %get-tuple-element.132, f32[512,4096]{1,0:T(8,128)S(1)} %fusion.37, f32[4096]{0:T(1024)S(1)} %get-tuple-element.129, f32[512]{0:T(512)S(1)} %bitcast.36), kind=kOutput, calls=%fused_computation.13.clone.1 | convolution fusion | flops 413138944 | bytes 8701956 | tf_op jit(solution)/shard_map/while/body/eval_jaxpr/ij,pj->pi/dot_general | solution.py:38
  205.7 6.7 %fusion.37 = f32[512,4096]{1,0:T(8,128)S(1)} fusion(f32[16,4096]{1,0:T(8,128)S(1)} %get-tuple-element.131, f32[8,16,512]{2,1,0:T(8,128)S(1)} %get-tuple-element.130, s32[]{:T(128)} %get-tuple-element.118), kind=kOutput, calls=%fused_computation.14.clone.1 | convolution fusion | flops 402653184 | bytes 8683524 | tf_op jit(solution)/shard_map/while/body/eval_jaxpr/fi,fj->ij/dot_general | solution.py:10
  212.4 9.0 %fusion.38 = f32[8,16,512]{2,1,0:T(8,128)S(1)} fusion(f32[8,16,512]{2,1,0:T(8,128)S(1)} %get-tuple-element.119, s32[]{:T(128)} %get-tuple-element.118, f32[16,4096]{1,0:T(8,128)S(1)} %get-tuple-element.132, f32[512,4096]{1,0:T(8,128)S(1)} %fusion.37, f32[4096]{0:T(1024)S(1)} %get-tuple-element.129, f32[512]{0:T(512)S(1)} %bitcast.36), kind=kOutput, calls=%fused_computation.13.clone.1 | convolution fusion | flops 413138944 | bytes 8701956 | tf_op jit(solution)/shard_map/while/body/eval_jaxpr/ij,pj->pi/dot_general | solution.py:38
  221.4 0.7 copy.11
  222.1 0.0 reduce-scatter.2.cloned.1.call-update
  222.2 0.1 multiply_reduce_fusion.4
  222.3 75.4 %reduce-scatter.2.cloned.1.call-done = f32[16,256]{1,0:T(8,128)} async-done(((f32[16,4096]{1,0:T(8,128)}), f32[16,256]{1,0:T(8,128)}) %reduce-scatter.2.cloned.1.call-update) | async-done | bytes 16400 | tf_op jit(solution)/shard_map/reduce_scatter | solution.py:42
  297.7 0.0 copy-done
  297.7 0.8 multiply_reduce_fusion.3
  298.6 75.7 %all-reduce = (f32[16]{0:T(128)S(1)}, f32[16]{0:T(128)S(1)}) all-reduce(f32[16]{0:T(128)S(1)} %multiply_reduce_fusion.4, f32[16]{0:T(128)S(1)} %multiply_reduce_fusion.3), channel_id=1, replica_groups=mesh['row'=16,'col'=16] {'row','col'}, use_global_device_ids=true, to_apply=%region_1.0 | all-reduce | flops 32 | bytes 256 | tf_op jit(solution)/shard_map/psum | solution.py:27
  374.3 0.9 multiply_reduce_fusion.2
  375.2 73.5 %psum.23 = f32[16]{0:T(128)S(1)} all-reduce(f32[16]{0:T(128)S(1)} %get-tuple-element.57), channel_id=1, replica_groups=mesh['row'=16,'col'=16] {'row','col'}, use_global_device_ids=true, to_apply=%region_10.11 | all-reduce | flops 16 | bytes 128 | tf_op jit(solution)/shard_map/psum | solution.py:46
  448.7 0.7 multiply_add_fusion
  (20 shorter events, 0.1 us)
Async XLA Ops:
  7.2 290.6 %reduce-scatter.2.cloned.1.call-start = ((), (), s32[]{:S(2)}) async-start(), calls=%async_computation.1 | async-start | bytes 278528 | tf_op jit(solution)/shard_map/reduce_scatter | solution.py:42
  95.6 126.6 %copy-start.1 = (f32[16,256]{1,0:T(8,128)S(1)}, f32[16,256]{1,0:T(8,128)}, u32[]{:S(2)}) copy-start(f32[16,256]{1,0:T(8,128)} %param.10) | copy-start | bytes 49156
  95.6 202.1 %copy-start = (f32[16,256]{1,0:T(8,128)S(1)}, f32[16,256]{1,0:T(8,128)}, u32[]{:S(2)}) copy-start(f32[16,256]{1,0:T(8,128)} %param.11) | copy-start | bytes 49156
  95.6 353.1 %copy-start.3 = (f32[16,256]{1,0:T(8,128)S(1)}, f32[16,256]{1,0:T(8,128)}, u32[]{:S(2)}) copy-start(f32[16,256]{1,0:T(8,128)} %param.9) | copy-start | bytes 49156
  375.2 74.2 %copy-start.2 = (f32[16,256]{1,0:T(8,128)}, f32[16,256]{1,0:T(8,128)S(1)}, u32[]{:S(2)}) copy-start(f32[16,256]{1,0:T(8,128)S(1)} %get-tuple-element.58) | copy-start | bytes 49156
Sparse Core Ops, SparseCore 0:
  222.3 75.3 reduce-scatter.1
where the time goes:
time: 457 us; the launch traced here: 456 us
  blocking collectives  237 us (52%)
  matrix products  126 us (28%)
  waiting for transfers between devices  75.4 us (16%)
  between operations  14.1 us (3%)
    psum x1, blocking collectives, on_device(): old_norm = lax.psum(jnp.sum(residual * residual, axis=1), ('row', 'col'))  75.7 us
    reduce_scatter x1, waiting for transfers between devices, on_device(): lax.psum_scatter(row_terms, 'col', scatter_dimension=1, tiled=True)  75.4 us
    psum x1, blocking collectives, on_device(): lax.psum(jnp.sum(new_residual * new_residual, axis=1), ('row', 'col'))  73.5 us
    dot_general x8, matrix products, one_block(): jnp.einsum('ij,pj->pi', kernel_tile, key_vecs, precision=lax.Precision.HI...  71.7 us
    dot_general x8, matrix products, kernel_tile_of(): jnp.einsum('fi,fj->ij', query, key_scaled, precision=lax.Precision.HIGHEST)  53.9 us
    all_gather x1, blocking collectives, on_device(): gathered = lax.all_gather(points, 'col', axis=1, tiled=True)  40.2 us
    all_gather x1, blocking collectives, on_device(): key_vecs = lax.all_gather(direction, 'row', axis=1, tiled=True)  24.4 us
    all_gather x1, blocking collectives, on_device(): key_points = lax.all_gather(points, 'row', axis=1, tiled=True)  22.9 us
  transfers between devices with their start and end apart: 1, of which 1 were waited for; matrix products, arithmetic and copies ran while one was open for 0% of the time, Pallas kernels for 0%

commit v1 on v0

v1 whole, which is shorter than its diff:
```python
import functools
import math

import jax
import jax.numpy as jnp
from jax import lax
from jax.experimental import pallas as pl
from jax.experimental.pallas import tpu as pltpu
from jax.sharding import PartitionSpec as P

MESH = pl.DeviceIdType.MESH
F32 = jnp.float32
BF16 = jnp.bfloat16
F8 = jnp.float8_e4m3fn

FEAT = 16
PROBES = 16
BLOCK = 256
GROUP = 16
PER = 4
CHUNK = PER * BLOCK
CHUNKS = GROUP // PER
DEPTH = 128
TOP = 17.0
DSCALE = 32.0
DZ = (0, 1, 7, 2, 6, 3, 5, 4)


def parts_of(values):
    high = values.astype(BF16).astype(F32)
    rest = values - high
    mid = rest.astype(BF16).astype(F32)
    return high, mid, (rest - mid).astype(BF16).astype(F32)


def features(points, factor, is_key):
    scaled = points * factor
    high, mid, low = parts_of(scaled)
    half = -0.5 * jnp.sum(scaled * scaled, axis=0, keepdims=True)
    if not is_key:
        half = half + TOP
    sq = parts_of(half)
    row = lax.broadcasted_iota(jnp.int32, (FEAT, BLOCK), 0)
    first = 0 if is_key else 3
    extra = jnp.where((row >= 3 - first) & (row < 6 - first), 1.0, 0.0)
    for i, part in enumerate(sq):
        extra = jnp.where(row == first + i, part, extra)
    if is_key:
        rows = [high, high, mid, high, mid, low, extra]
    else:
        rows = [high, mid, high, low, mid, high, extra]
    return jnp.concatenate(rows + [jnp.zeros((FEAT, BLOCK), F32)], axis=0)


def cg_kernel(
    points_hbm, factor_ref, sol_hbm, res_hbm, dir_hbm,
    new_sol_ref, new_res_ref, new_dir_ref,
    own, sol, res, kbuf, qbuf, kf, qf, db, d8, xs, hs, ls, acc_h, acc_l,
    rs_out, rs_in, ar1_out, ar1_in, ar2_out, ar2_in,
    in_sem, k_send, k_recv, f_send, q_send, q_recv, rs_send, rs_recv, a1_send, a1_recv, a2_send, a2_recv,
):
    row, col = lax.axis_index("row"), lax.axis_index("col")
    y, z_lo, core = row // 4, (row // 2) % 2, row % 2
    x, z = col // 4, (col % 4) * 2 + z_lo

    def plane(dx, dy):
        return (lax.rem(y + dy, 4) * 4 + z_lo * 2 + core, lax.rem(x + dx, 4) * 4 + col % 4)

    def pillar(dz, other):
        to_z = lax.rem(z + dz, 8)
        to_core = 1 - core if other else core
        return (y * 4 + (to_z % 2) * 2 + to_core, x * 4 + to_z // 2)

    def remote(src, dst, send, recv, device):
        return pltpu.make_async_remote_copy(
            src_ref=src, dst_ref=dst, send_sem=send, recv_sem=recv, device_id=device, device_id_type=MESH
        )

    loads = [
        pltpu.make_async_copy(points_hbm, own.at[pl.ds(0, FEAT)], in_sem.at[0]),
        pltpu.make_async_copy(dir_hbm, own.at[pl.ds(FEAT, PROBES)], in_sem.at[1]),
        pltpu.make_async_copy(sol_hbm, sol, in_sem.at[2]),
        pltpu.make_async_copy(res_hbm, res, in_sem.at[3]),
    ]
    for load in loads:
        load.start()

    barrier = pltpu.get_barrier_semaphore()
    for s in range(1, GROUP):
        pl.semaphore_signal(barrier, inc=1, device_id=plane(s // 4, s % 4), device_id_type=MESH)
        pl.semaphore_signal(barrier, inc=1, device_id=pillar(s // 2, s % 2), device_id_type=MESH)
    for load in loads:
        load.wait()
    pl.semaphore_wait(barrier, 2 * (GROUP - 1))

    q_copies, k_copies = {}, {}
    k_copies[1] = remote(own, kbuf.at[1], k_send.at[1], k_recv.at[1], pillar(0, 1))
    for i, dz in enumerate(DZ):
        if i:
            k_copies[2 * i] = remote(own, kbuf.at[2 * i], k_send.at[2 * i], k_recv.at[2 * i], pillar(dz, 0))
    for s in range(1, GROUP):
        q_copies[s] = remote(
            own.at[pl.ds(0, FEAT)], qbuf.at[s], q_send.at[s], q_recv.at[s], plane(s // 4, s % 4)
        )
    k_copies[1].start()
    for s in range(1, GROUP):
        q_copies[s].start()
        if s % 2 == 0:
            k_copies[s].start()

    def forward(slot):
        return remote(kbuf.at[slot], kbuf.at[slot + 1], f_send.at[slot], k_recv.at[slot + 1], pillar(0, 1))

    factor = factor_ref[...]

    def prep_key(slot, source):
        kf[slot * BLOCK:(slot + 1) * BLOCK, :] = features(source[0:FEAT], factor, True).T.astype(BF16)
        vec = source[FEAT:FEAT + PROBES]
        high = vec.astype(BF16).astype(F32)
        db[:, slot * BLOCK:(slot + 1) * BLOCK] = jnp.concatenate([high, vec - high], axis=0).astype(BF16)
        wide = vec * DSCALE
        first = wide.astype(F8).astype(F32)
        d8[:, slot * BLOCK:(slot + 1) * BLOCK] = jnp.concatenate([first, wide - first], axis=0).astype(F8)

    def relay_chunk(chunk):
        for slot in range(chunk * PER, (chunk + 1) * PER, 2):
            if slot:
                k_copies[slot].wait_recv()
                forward(slot).start()

    def prep_key_chunk(chunk):
        for slot in range(chunk * PER, (chunk + 1) * PER):
            if slot == 0:
                prep_key(0, own)
                continue
            if slot % 2:
                k_copies[1].wait_recv() if slot == 1 else forward(slot - 1).wait_recv()
            prep_key(slot, kbuf.at[slot])

    def prep_query(slot, source):
        lanes = pl.ds(pl.multiple_of(slot * BLOCK, BLOCK), BLOCK)
        qf[:, lanes] = features(source, factor, False).astype(BF16)

    def prep_query_chunk(chunk):
        def one(i, carry):
            slot = chunk * PER + i
            remote(
                own.at[pl.ds(0, FEAT)], qbuf.at[slot], q_send.at[slot], q_recv.at[slot], plane(0, 0)
            ).wait_recv()
            prep_query(slot, qbuf[slot])
            return carry
        lax.fori_loop(0, PER, one, 0)

    def exponents(q, k, at):
        lanes = pl.ds(pl.multiple_of(q * CHUNK, CHUNK), CHUNK)
        xs[at][...] = jnp.dot(kf[k * CHUNK:(k + 1) * CHUNK, :], qf[:, lanes], preferred_element_type=F32)

    def entries(at):
        value = jnp.exp2(jnp.minimum(xs[at][...], TOP))
        high = value.astype(BF16)
        hs[at][...] = high
        ls[at][...] = (value - high.astype(F32)).astype(F8)

    def products(k, at):
        keys = slice(k * CHUNK, (k + 1) * CHUNK)
        high = jnp.dot(db[:, keys], hs[at][...], preferred_element_type=F32)
        low = jnp.dot(d8[:, keys], ls[at][...], preferred_element_type=F32)
        if k == 0:
            acc_h[...] = high
            acc_l[...] = low
        else:
            acc_h[...] += high
            acc_l[...] += low

    def image_chunk():
        low = (acc_l[0:PROBES] + acc_l[PROBES:2 * PROBES]) * (1.0 / DSCALE)
        return (acc_h[0:PROBES] + acc_h[PROBES:2 * PROBES] + low) * (2.0 ** -TOP)

    def give(slot, device):
        return remote(rs_out.at[slot], rs_in.at[slot], rs_send.at[slot], rs_recv.at[slot], device)

    def send_chunk(q, first):
        image = image_chunk()
        for i in range(PER):
            rs_out[q * PER + i] = image[:, i * BLOCK:(i + 1) * BLOCK]
        for i in range(first, PER):
            slot = q * PER + i
            give(slot, plane(4 - q, (4 - i) % 4)).start()

    relay_chunk(0)
    prep_key_chunk(0)
    prep_query(0, own[0:FEAT])
    for s in range(1, PER):
        q_copies[s].wait_recv()
        prep_query(s, qbuf[s])
    exponents(0, 0, 0)
    relay_chunk(1)
    for k in range(CHUNKS):
        if k + 1 < CHUNKS:
            if k + 2 < CHUNKS:
                relay_chunk(k + 2)
            prep_key_chunk(k + 1)
            exponents(0, k + 1, (k + 1) % 2)
        else:
            prep_query_chunk(1)
            exponents(1, 0, 0)
        entries(k % 2)
        if k:
            products(k - 1, (k - 1) % 2)

    def query_chunk(q, carry):
        exponents(q, 1, 1)
        entries(0)
        products(CHUNKS - 1, (CHUNKS - 1) % 2)

        @pl.when(q == 1)
        def _():
            send_chunk(0, 1)

        @pl.when(q > 1)
        def _():
            send_chunk(q - 1, 0)

        for k in range(1, CHUNKS - 1):
            exponents(q, k + 1, (k + 1) % 2)
            entries(k % 2)
            products(k - 1, (k - 1) % 2)

        @pl.when(q + 1 < CHUNKS)
        def _():
            prep_query_chunk(q + 1)
            exponents(q + 1, 0, 0)

        entries((CHUNKS - 1) % 2)
        products(CHUNKS - 2, (CHUNKS - 2) % 2)
        return carry

    lax.fori_loop(1, CHUNKS, query_chunk, 0)
    products(CHUNKS - 1, (CHUNKS - 1) % 2)
    send_chunk(CHUNKS - 1, 0)

    image = rs_out[0]
    for s in range(1, GROUP):
        give(s, plane(0, 0)).wait_recv()
        image = image + rs_in[s]

    vec, resid = own[FEAT:FEAT + PROBES], res[...]
    lane = lax.broadcasted_iota(jnp.int32, (PROBES, 128), 1)
    sums = jnp.zeros((PROBES, 128), F32)
    for i, (left, right) in enumerate(((resid, resid), (vec, image), (resid, image), (image, image))):
        sums = jnp.where(lane == i, jnp.sum(left * right, axis=1, keepdims=True), sums)

    def all_sum(value, out, into, send, recv, peer):
        out[...] = value
        copies = [
            remote(out, into.at[s], send.at[s], recv.at[s], peer(s)) for s in range(1, GROUP)
        ]
        for copy in copies:
            copy.start()
        for s, copy in enumerate(copies, 1):
            copy.wait_recv()
            value = value + into[s]
        return value, copies

    sums, a1 = all_sum(sums, ar1_out, ar1_in, a1_send, a1_recv, lambda s: plane(s // 4, s % 4))
    sums, a2 = all_sum(sums, ar2_out, ar2_in, a2_send, a2_recv, lambda s: pillar(s // 2, s % 2))

    old_norm, curvature, cross, square = (sums[:, i:i + 1] for i in range(4))
    step = old_norm / curvature
    new_norm = old_norm - 2.0 * step * cross + step * step * square
    new_res = resid - step * image
    new_sol_ref[...] = sol[...] + step * vec
    new_res_ref[...] = new_res
    new_dir_ref[...] = new_res + (new_norm / old_norm) * vec

    for s in range(1, GROUP):
        q_copies[s].wait_send()
        give(s, plane(0, 0)).wait_send()
    for slot, copy in k_copies.items():
        copy.wait_send()
    for slot in range(2, GROUP, 2):
        forward(slot).wait_send()
    for copy in a1 + a2:
        copy.wait_send()


def on_device(points, inv_length, solution_, residual, direction):
    factor = jnp.broadcast_to((inv_length * math.sqrt(math.log2(math.e)))[:, None], (FEAT, BLOCK))
    shape = jax.ShapeDtypeStruct((PROBES, BLOCK), F32)
    vmem, hbm = pl.BlockSpec(memory_space=pltpu.VMEM), pl.BlockSpec(memory_space=pl.ANY)
    dma = pltpu.SemaphoreType.DMA
    return pl.pallas_call(
        lambda *refs: cg_kernel(*refs[:17], refs[17:19], refs[19:21], refs[21:23], *refs[23:]),
        out_shape=(shape, shape, shape),
        in_specs=[hbm, vmem, hbm, hbm, hbm],
        out_specs=(vmem, vmem, vmem),
        scratch_shapes=[
            pltpu.VMEM((FEAT + PROBES, BLOCK), F32),
            pltpu.VMEM((PROBES, BLOCK), F32),
            pltpu.VMEM((PROBES, BLOCK), F32),
            pltpu.VMEM((GROUP, FEAT + PROBES, BLOCK), F32),
            pltpu.VMEM((GROUP, FEAT, BLOCK), F32),
            pltpu.VMEM((GROUP * BLOCK, DEPTH), BF16),
            pltpu.VMEM((DEPTH, GROUP * BLOCK), BF16),
            pltpu.VMEM((2 * PROBES, GROUP * BLOCK), BF16),
            pltpu.VMEM((2 * PROBES, GROUP * BLOCK), F8),
        ]
        + [pltpu.VMEM((CHUNK, CHUNK), F32)] * 2
        + [pltpu.VMEM((CHUNK, CHUNK), BF16)] * 2
        + [pltpu.VMEM((CHUNK, CHUNK), F8)] * 2
        + [
            pltpu.VMEM((2 * PROBES, CHUNK), F32),
            pltpu.VMEM((2 * PROBES, CHUNK), F32),
            pltpu.VMEM((GROUP, PROBES, BLOCK), F32),
            pltpu.VMEM((GROUP, PROBES, BLOCK), F32),
            pltpu.VMEM((PROBES, 128), F32),
            pltpu.VMEM((GROUP, PROBES, 128), F32),
            pltpu.VMEM((PROBES, 128), F32),
            pltpu.VMEM((GROUP, PROBES, 128), F32),
            dma((4,)),
        ]
        + [dma((GROUP,))] * 11,
        compiler_params=pltpu.CompilerParams(
            collective_id=0, has_side_effects=True, vmem_limit_bytes=48 * 2**20
        ),
    )(points, factor, solution_, residual, direction)


def solution(mesh):
    split = P(None, ("row", "col"))
    return jax.shard_map(
        on_device,
        mesh=mesh,
        in_specs=(split, P(), split, split, split),
        out_specs=(split, split, split),
        check_vma=False,
    )
```

time: 457 us -> 74.7 us (0.16)
  blocking collectives: 237 us -> 0 us
  matrix products: 126 us -> 0 us
  waiting for transfers between devices: 75.4 us -> 0 us
  Pallas kernels: 0 us -> 68.9 us
  between operations: 14.1 us -> 0.65 us
    psum x2 -> x0, blocking collectives: 149 us -> none  [the longest x1 75.7 us: on_device(): old_norm = lax.psum(jnp.sum(residual * residual, axis=1), ('row', 'col'))]
    dot_general x16 -> x0, matrix products: 126 us -> none  [the longest x8 71.7 us: one_block(): jnp.einsum('ij,pj->pi', kernel_tile, key_vecs, precision=lax.Precision.HI...]
    all_gather x3 -> x0, blocking collectives: 87.5 us -> none  [the longest x1 40.2 us: on_device(): gathered = lax.all_gather(points, 'col', axis=1, tiled=True)]
    reduce_scatter x1 -> x0, waiting for transfers between devices: 75.4 us -> none  [on_device(): lax.psum_scatter(row_terms, 'col', scatter_dimension=1, tiled=True)]
    pallas_call x0 -> x1, Pallas kernels: none -> 68.9 us  [on_device(): pl.pallas_call(lambda *refs: cg_kernel(*refs[:17], refs[17:19], refs[19:2...]
  transfers between devices with their start and end apart: 1 -> 0, of which waited for: 1 -> 0; matrix products, arithmetic and copies ran while one was open for 0% -> 0% of each run, Pallas kernels for 0% -> 0%
where the time goes in v1:
time: 74.7 us; the launch traced here: 74.3 us
  Pallas kernels  68.9 us (92%)
  local copies, waits for them, and re-layouts  4.05 us (5%)
    pallas_call x1, Pallas kernels, on_device(): pl.pallas_call(lambda *refs: cg_kernel(*refs[:17], refs[17:19], refs[19:2...  68.9 us
    unnamed x11, local copies, waits for them, and re-layouts  3.97 us

profile of v1, /device:TPU:1, one launch (start us, length us, event | category | flops | bytes accessed | tf_op | source)
XLA Modules:
  0.0 74.3 jit_solution(10977161204966757168)
XLA Ops:
  0.6 0.0 copy-start
  0.6 0.7 broadcast_multiply_fusion
  1.3 0.1 broadcast_in_dim.2.refs_1_
  1.4 0.0 copy-done
  1.4 0.0 copy-start.1
  1.4 0.7 copy-done.1
  2.1 0.0 copy-start.2
  2.1 0.7 copy-done.2
  2.8 0.0 copy-start.3
  2.8 0.7 copy-done.3
  3.5 68.9 %shard_map.76 = (f32[16,256]{1,0:T(8,128)S(1)}, f32[16,256]{1,0:T(8,128)S(1)}, f32[16,256]{1,0:T(8,128)S(1)}) custom-call(f32[16,256]{1,0:T(8,128)S(1)} %copy-done, f32[16,256]{1,0:T(8,128)S(1)} %broadcast_in_dim.2.refs_1_, f32[16,256]{1,0:T(8,128)S(1)} %copy-done.1, f32[16,256]{1,0:T(8,128)S(1)} %copy-done.2, f32[16,256]{1,0:T(8,128)S(1)} %copy-done.3), custom_call_target="tpu_custom_call" | custom-call | tf_op jit(solution)/shard_map/pallas_call | solution.py:292
  72.4 0.6 copy.11
  73.0 0.6 copy.12
  73.7 0.6 copy.13
Async XLA Ops:
  0.6 0.7 %copy-start = (f32[16,256]{1,0:T(8,128)S(1)}, f32[16,256]{1,0:T(8,128)}, u32[]{:S(2)}) copy-start(f32[16,256]{1,0:T(8,128)} %refs_0_.1) | copy-start | bytes 49156
  1.4 0.7 copy-start.1
  2.1 0.7 copy-start.2
  2.8 0.7 copy-start.3

commit v2 on v1

v2 whole, which is shorter than its diff:
```python
import functools
import math

import jax
import jax.numpy as jnp
from jax import lax
from jax.experimental import pallas as pl
from jax.experimental.pallas import tpu as pltpu
from jax.sharding import PartitionSpec as P

MESH = pl.DeviceIdType.MESH
F32 = jnp.float32
BF16 = jnp.bfloat16
F8 = jnp.float8_e4m3fn

FEAT = 16
PROBES = 16
BLOCK = 256
GROUP = 16
KPER = 4
KCHUNK = KPER * BLOCK
KCHUNKS = GROUP // KPER
QPER = 2
QCHUNK = QPER * BLOCK
QCHUNKS = GROUP // QPER
VMEM_LIMIT = 60 * 2**20
DEPTH = 128
TOP = 17.0
DSCALE = 32.0
DZ = (0, 1, 7, 2, 6, 3, 5, 4)


def parts_of(values):
    high = values.astype(BF16).astype(F32)
    rest = values - high
    mid = rest.astype(BF16).astype(F32)
    return high, mid, (rest - mid).astype(BF16).astype(F32)


def features(points, factor, is_key):
    scaled = points * factor
    high, mid, low = parts_of(scaled)
    half = -0.5 * jnp.sum(scaled * scaled, axis=0, keepdims=True)
    if not is_key:
        half = half + TOP
    sq = parts_of(half)
    row = lax.broadcasted_iota(jnp.int32, (FEAT, BLOCK), 0)
    first = 0 if is_key else 3
    extra = jnp.where((row >= 3 - first) & (row < 6 - first), 1.0, 0.0)
    for i, part in enumerate(sq):
        extra = jnp.where(row == first + i, part, extra)
    if is_key:
        rows = [high, high, mid, high, mid, low, extra]
    else:
        rows = [high, mid, high, low, mid, high, extra]
    return jnp.concatenate(rows + [jnp.zeros((FEAT, BLOCK), F32)], axis=0)


def cg_kernel(
    points_hbm, inverse_ref, res_hbm, dir_hbm,
    image_ref, step_ref, ratio_ref,
    own, res, kbuf, qbuf, kf, qf, db, d8, xs, hs, ls, acc,
    rs_out, rs_in, ar1, ar2,
    in_sem, k_send, k_recv, f_send, q_send, q_recv, rs_send, rs_recv, a1_send, a1_recv, a2_send, a2_recv,
):
    row, col = lax.axis_index("row"), lax.axis_index("col")
    y, z_lo, core = row // 4, (row // 2) % 2, row % 2
    x, z = col // 4, (col % 4) * 2 + z_lo

    def plane(dx, dy):
        return (lax.rem(y + dy, 4) * 4 + z_lo * 2 + core, lax.rem(x + dx, 4) * 4 + col % 4)

    def pillar(dz, other):
        to_z = lax.rem(z + dz, 8)
        to_core = 1 - core if other else core
        return (y * 4 + (to_z % 2) * 2 + to_core, x * 4 + to_z // 2)

    def remote(src, dst, send, recv, device):
        return pltpu.make_async_remote_copy(
            src_ref=src, dst_ref=dst, send_sem=send, recv_sem=recv, device_id=device, device_id_type=MESH
        )

    loads = [
        pltpu.make_async_copy(points_hbm, own.at[pl.ds(0, FEAT)], in_sem.at[0]),
        pltpu.make_async_copy(dir_hbm, own.at[pl.ds(FEAT, PROBES)], in_sem.at[1]),
        pltpu.make_async_copy(res_hbm, res, in_sem.at[2]),
    ]
    for load in loads:
        load.start()

    barrier = pltpu.get_barrier_semaphore()
    for s in range(1, GROUP):
        pl.semaphore_signal(barrier, inc=1, device_id=plane(s // 4, s % 4), device_id_type=MESH)
        pl.semaphore_signal(barrier, inc=1, device_id=pillar(s // 2, s % 2), device_id_type=MESH)
    for load in loads:
        load.wait()
    pl.semaphore_wait(barrier, 2 * (GROUP - 1))

    q_copies, k_copies = {}, {}
    k_copies[1] = remote(own, kbuf.at[1], k_send.at[1], k_recv.at[1], pillar(0, 1))
    for i, dz in enumerate(DZ):
        if i:
            k_copies[2 * i] = remote(own, kbuf.at[2 * i], k_send.at[2 * i], k_recv.at[2 * i], pillar(dz, 0))
    for s in range(1, GROUP):
        q_copies[s] = remote(
            own.at[pl.ds(0, FEAT)], qbuf.at[s], q_send.at[s], q_recv.at[s], plane(s // 4, s % 4)
        )
    k_copies[1].start()
    k_copies[2].start()
    k_copies[4].start()
    for s in range(1, GROUP):
        q_copies[s].start()
        if s % 2 and 6 <= s + 5 < GROUP:
            k_copies[s + 5].start()

    def forward(slot):
        return remote(kbuf.at[slot], kbuf.at[slot + 1], f_send.at[slot], k_recv.at[slot + 1], pillar(0, 1))

    at_row = lax.broadcasted_iota(jnp.int32, (FEAT, FEAT), 0)
    at_lane = lax.broadcasted_iota(jnp.int32, (FEAT, FEAT), 1)
    factor = jnp.sum(jnp.where(at_row == at_lane, inverse_ref[...], 0.0), axis=1, keepdims=True)
    factor = factor * math.sqrt(math.log2(math.e))

    def prep_key(slot, source):
        kf[slot * BLOCK:(slot + 1) * BLOCK, :] = features(source[0:FEAT], factor, True).T.astype(BF16)
        vec = source[FEAT:FEAT + PROBES]
        high = vec.astype(BF16).astype(F32)
        db[:, slot * BLOCK:(slot + 1) * BLOCK] = jnp.concatenate([high, vec - high], axis=0).astype(BF16)
        wide = vec * DSCALE
        first = wide.astype(F8).astype(F32)
        d8[:, slot * BLOCK:(slot + 1) * BLOCK] = jnp.concatenate([first, wide - first], axis=0).astype(F8)

    def relay_chunk(chunk):
        for slot in range(chunk * KPER, (chunk + 1) * KPER, 2):
            if slot:
                k_copies[slot].wait_recv()
                forward(slot).start()

    def prep_key_chunk(chunk, skip):
        for slot in range(chunk * KPER + skip, (chunk + 1) * KPER):
            if slot % 2:
                k_copies[1].wait_recv() if slot == 1 else forward(slot - 1).wait_recv()
            prep_key(slot, kbuf.at[slot])

    def prep_query(slot, source):
        lanes = pl.ds(pl.multiple_of(slot * BLOCK, BLOCK), BLOCK)
        qf[:, lanes] = features(source, factor, False).astype(BF16)

    def exponents(q, k, at):
        lanes = pl.ds(pl.multiple_of(q * QCHUNK, QCHUNK), QCHUNK)
        xs[at][...] = jnp.dot(kf[k * KCHUNK:(k + 1) * KCHUNK, :], qf[:, lanes], preferred_element_type=F32)

    def entries(at):
        value = jnp.exp2(jnp.minimum(xs[at][...], TOP))
        high = value.astype(BF16)
        hs[at][...] = high
        ls[at][...] = (value - high.astype(F32)).astype(F8)

    def products(k, at):
        keys = slice(k * KCHUNK, (k + 1) * KCHUNK)
        high = jnp.dot(db[:, keys], hs[at][...], preferred_element_type=F32)
        low = jnp.dot(d8[:, keys], ls[at][...], preferred_element_type=F32)
        return high + low * (1.0 / DSCALE)

    def block(q, half):
        k = 2 * half
        exponents(q, k, 0)
        exponents(q, k + 1, 1)
        entries(0)
        first = products(k, 0)
        entries(1)
        return first + products(k + 1, 1)

    def give(slot, device):
        return remote(rs_out.at[slot], rs_in.at[slot], rs_send.at[slot], rs_recv.at[slot], device)

    relay_chunk(0)
    relay_chunk(1)
    prep_key(0, own)
    prep_query(0, own[0:FEAT])
    prep_key_chunk(0, 1)
    for s in range(1, QPER):
        q_copies[s].wait_recv()
        prep_query(s, qbuf[s])
    prep_key_chunk(1, 0)
    acc[0] = block(0, 0)

    def first_half(q, carry):
        for i in range(QPER):
            slot = q * QPER + i
            remote(
                own.at[pl.ds(0, FEAT)], qbuf.at[slot], q_send.at[slot], q_recv.at[slot], plane(0, 0)
            ).wait_recv()
        for i in range(QPER):
            prep_query(q * QPER + i, qbuf[q * QPER + i])

        @pl.when(q == QCHUNKS // 2)
        def _():
            relay_chunk(2)

        @pl.when(q == QCHUNKS - 2)
        def _():
            relay_chunk(3)

        acc[q] = block(q, 0)
        return carry

    lax.fori_loop(1, QCHUNKS, first_half, 0)
    prep_key_chunk(2, 0)
    prep_key_chunk(3, 0)

    def second_half(i, carry):
        q = QCHUNKS - 1 - i
        total = acc[q] + block(q, 1)
        image = (total[0:PROBES] + total[PROBES:2 * PROBES]) * (2.0 ** -TOP)
        for j in range(QPER):
            rs_out[q * QPER + j] = image[:, j * BLOCK:(j + 1) * BLOCK]
        for j in range(QPER):
            slot = q * QPER + j

            @pl.when(slot > 0)
            def _():
                give(slot, plane(4 - slot // 4, 4 - slot % 4)).start()

        return carry

    lax.fori_loop(0, QCHUNKS, second_half, 0)

    image = rs_out[0]
    for s in range(1, GROUP):
        give(s, plane(0, 0)).wait_recv()
        image = image + rs_in[s]

    vec, resid = own[FEAT:FEAT + PROBES], res[...]
    image_ref[...] = image
    terms = [resid * resid, vec * image, resid * image, image * image]
    terms = jnp.concatenate([term[:, :128] + term[:, 128:] for term in terms] * 2, axis=0)
    sums = jnp.sum(terms.T, axis=0, keepdims=True)

    def all_sum(value, into, send, recv, peer):
        into[0:1] = value
        copies = [
            remote(into.at[pl.ds(0, 1)], into.at[pl.ds(s, 1)], send.at[s], recv.at[s], peer(s))
            for s in reversed(range(1, GROUP))
        ]
        for copy in copies:
            copy.start()
        for copy in copies:
            copy.wait_recv()
        return jnp.sum(into[...], axis=0, keepdims=True), copies

    sums, a1 = all_sum(sums, ar1, a1_send, a1_recv, lambda s: plane(s // 4, s % 4))
    sums, a2 = all_sum(sums, ar2, a2_send, a2_recv, lambda s: pillar(s // 2, s % 2))

    columns = jnp.broadcast_to(sums, (BLOCK, 128)).T
    old_norm, curvature, cross, square = (columns[i * PROBES:(i + 1) * PROBES] for i in range(4))
    step = old_norm / curvature
    new_norm = old_norm - 2.0 * step * cross + step * step * square
    step_ref[...] = step
    ratio_ref[...] = new_norm / old_norm

    for s in range(1, GROUP):
        q_copies[s].wait_send()
        give(s, plane(0, 0)).wait_send()
    for slot, copy in k_copies.items():
        copy.wait_send()
    for slot in range(2, GROUP, 2):
        forward(slot).wait_send()
    for copy in a1 + a2:
        copy.wait_send()


def on_device(points, inv_length, solution_, residual, direction):
    vmem, hbm = pl.BlockSpec(memory_space=pltpu.VMEM), pl.BlockSpec(memory_space=pl.ANY)
    dma = pltpu.SemaphoreType.DMA
    image, step, ratio = pl.pallas_call(
        lambda *refs: cg_kernel(*refs[:15], refs[15:17], refs[17:19], refs[19:21], *refs[21:]),
        out_shape=(jax.ShapeDtypeStruct((PROBES, BLOCK), F32),) * 3,
        in_specs=[hbm, vmem, hbm, hbm],
        out_specs=(vmem, vmem, vmem),
        scratch_shapes=[
            pltpu.VMEM((FEAT + PROBES, BLOCK), F32),
            pltpu.VMEM((PROBES, BLOCK), F32),
            pltpu.VMEM((GROUP, FEAT + PROBES, BLOCK), F32),
            pltpu.VMEM((GROUP, FEAT, BLOCK), F32),
            pltpu.VMEM((GROUP * BLOCK, DEPTH), BF16),
            pltpu.VMEM((DEPTH, GROUP * BLOCK), BF16),
            pltpu.VMEM((2 * PROBES, GROUP * BLOCK), BF16),
            pltpu.VMEM((2 * PROBES, GROUP * BLOCK), F8),
        ]
        + [pltpu.VMEM((KCHUNK, QCHUNK), F32)] * 2
        + [pltpu.VMEM((KCHUNK, QCHUNK), BF16)] * 2
        + [pltpu.VMEM((KCHUNK, QCHUNK), F8)] * 2
        + [
            pltpu.VMEM((QCHUNKS, 2 * PROBES, QCHUNK), F32),
            pltpu.VMEM((GROUP, PROBES, BLOCK), F32),
            pltpu.VMEM((GROUP, PROBES, BLOCK), F32),
            pltpu.VMEM((GROUP, 128), F32),
            pltpu.VMEM((GROUP, 128), F32),
            dma((3,)),
        ]
        + [dma((GROUP,))] * 11,
        compiler_params=pltpu.CompilerParams(
            collective_id=0, has_side_effects=True, vmem_limit_bytes=VMEM_LIMIT
        ),
    )(points, inv_length[None, :], residual, direction)
    new_residual = residual - step * image
    return solution_ + step * direction, new_residual, new_residual + ratio * direction


def solution(mesh):
    split = P(None, ("row", "col"))
    return jax.shard_map(
        on_device,
        mesh=mesh,
        in_specs=(split, P(), split, split, split),
        out_specs=(split, split, split),
        check_vma=False,
    )
```

time: 74.7 us -> 56.8 us (0.76)
  Pallas kernels: 68.9 us -> 54.4 us
  local copies, waits for them, and re-layouts: 4.05 us -> 0.01 us
    pallas_call x1, Pallas kernels: 68.9 us -> 54.4 us  [on_device(): pl.pallas_call(lambda *refs: cg_kernel(*refs[:15], refs[15:17], refs[17:1...]
    unnamed x11 -> x6, local copies, waits for them, and re-layouts: 3.97 us -> 0.01 us
    add x0 -> x1, other arithmetic: none -> 1.38 us  [on_device(): new_residual + ratio * direction]
where the time goes in v2:
time: 56.8 us; the launch traced here: 56.5 us
  Pallas kernels  54.4 us (96%)
  other arithmetic  1.38 us (2%)
  between operations  0.69 us (1%)
    pallas_call x1, Pallas kernels, on_device(): pl.pallas_call(lambda *refs: cg_kernel(*refs[:15], refs[15:17], refs[17:1...  54.4 us
    add x1, other arithmetic, on_device(): new_residual + ratio * direction  1.38 us

profile of v2, /device:TPU:1, one launch (start us, length us, event | category | flops | bytes accessed | tf_op | source)
XLA Modules:
  0.0 56.5 jit_solution(8248084654730829306)
XLA Ops:
  0.6 0.0 copy-start
  0.6 0.0 copy-start.1
  0.7 0.0 copy-start.2
  0.7 54.4 %shard_map.76 = (f32[16,256]{1,0:T(8,128)}, f32[16,256]{1,0:T(8,128)}, f32[16,256]{1,0:T(8,128)}) custom-call(f32[16,256]{1,0:T(8,128)} %refs_0_.1, f32[1,16]{1,0:T(1,128)} %bitcast.1, f32[16,256]{1,0:T(8,128)} %refs_2_.1, f32[16,256]{1,0:T(8,128)} %refs_3_.1), custom_call_target="tpu_custom_call" | custom-call | tf_op jit(solution)/shard_map/pallas_call | solution.py:276
  55.1 0.0 copy-done
  55.1 0.0 copy-done.1
  55.1 0.0 copy-done.2
  55.1 1.4 %multiply_add_fusion = (f32[16,256]{1,0:T(8,128)}, f32[16,256]{1,0:T(8,128)}, f32[16,256]{1,0:T(8,128)}) fusion(f32[16,256]{1,0:T(8,128)} %get-tuple-element.8, f32[16,256]{1,0:T(8,128)S(1)} %copy-done.1, f32[16,256]{1,0:T(8,128)S(1)} %copy-done, f32[16,256]{1,0:T(8,128)} %get-tuple-element.6, f32[16,256]{1,0:T(8,128)} %get-tuple-element.7, ...), kind=kLoop, calls=%fused_computation | loop fusion | flops 24576 | bytes 147456 | tf_op jit(solution)/shard_map/add | solution.py:308
Async XLA Ops:
  0.6 54.4 %copy-start = (f32[16,256]{1,0:T(8,128)S(1)}, f32[16,256]{1,0:T(8,128)}, u32[]{:S(2)}) copy-start(f32[16,256]{1,0:T(8,128)} %refs_2_.1) | copy-start | bytes 49156
  0.6 54.4 %copy-start.1 = (f32[16,256]{1,0:T(8,128)S(1)}, f32[16,256]{1,0:T(8,128)}, u32[]{:S(2)}) copy-start(f32[16,256]{1,0:T(8,128)} %refs_3_.1) | copy-start | bytes 49156
  0.7 54.4 %copy-start.2 = (f32[16,256]{1,0:T(8,128)S(1)}, f32[16,256]{1,0:T(8,128)}, u32[]{:S(2)}) copy-start(f32[16,256]{1,0:T(8,128)} %param.7) | copy-start | bytes 49156

commit v3 on v2

v3 whole, which is shorter than its diff:
```python
import functools
import math

import jax
import jax.numpy as jnp
from jax import lax
from jax.experimental import pallas as pl
from jax.experimental.pallas import tpu as pltpu
from jax.sharding import PartitionSpec as P

MESH = pl.DeviceIdType.MESH
F32 = jnp.float32
BF16 = jnp.bfloat16
F8 = jnp.float8_e4m3fn

FEAT = 16
PROBES = 16
BLOCK = 256
GROUP = 16
CHIPS = 128
KPER = 4
KCHUNK = KPER * BLOCK
KCHUNKS = GROUP // KPER
QPER = 2
QCHUNK = QPER * BLOCK
QCHUNKS = GROUP // QPER
VMEM_LIMIT = 60 * 2**20
RELAYS_FIRST = ((2, (6,)), (3, (12,)))
RELAYS_SECOND = ((0, (8, 10)), (2, (14,)))
DEPTH = 128
TOP = 17.0
DSCALE = 32.0
KEYS = ((0, 0), (0, 1), (1, 0), (7, 0), (1, 1), (7, 1), (2, 0), (2, 1), (6, 0), (6, 1), (3, 0), (3, 1), (5, 0), (5, 1), (4, 0), (4, 1))
FAR = KEYS.index((4, 0))
RELAYED = {KEYS.index((dz, 0)): KEYS.index((dz, 1)) for dz in range(1, 8)}


def parts_of(values):
    high = values.astype(BF16)
    rest = values - high.astype(F32)
    mid = rest.astype(BF16)
    return high, mid, (rest - mid.astype(F32)).astype(BF16)


def features(points, factor, is_key):
    scaled = points * factor
    high, mid, low = parts_of(scaled)
    half = -0.5 * jnp.sum(scaled * scaled, axis=0, keepdims=True)
    if not is_key:
        half = half + TOP
    row = lax.broadcasted_iota(jnp.int32, (FEAT, BLOCK), 0)
    first = 0 if is_key else 3
    extra = jnp.where((row >= 3 - first) & (row < 6 - first), 1.0, 0.0)
    for i, part in enumerate(parts_of(half)):
        extra = jnp.where(row == first + i, part.astype(F32), extra)
    extra = extra.astype(BF16)
    blank = jnp.zeros((FEAT, BLOCK), BF16)
    if is_key:
        return [high, high, mid, high, mid, low, extra, blank]
    return [high, mid, high, low, mid, high, extra, blank]


def cg_kernel(
    points_hbm, inverse_ref, res_hbm, dir_hbm,
    image_ref, step_ref, ratio_ref,
    own, res, kbuf, qbuf, kf, qf, db, d8, xs, hs, ls, acc,
    rs_out, rs_in, pair, chips,
    in_sem, k_send, k_recv, f_send, q_send, q_recv, rs_send, rs_recv, a1_send, a1_recv, a2_send, a2_recv,
):
    row, col = lax.axis_index("row"), lax.axis_index("col")
    y, z_lo, core = row // 4, (row // 2) % 2, row % 2
    x, z = col // 4, (col % 4) * 2 + z_lo

    def plane(dx, dy):
        return (lax.rem(y + dy, 4) * 4 + z_lo * 2 + core, lax.rem(x + dx, 4) * 4 + col % 4)

    def near(i):
        return i + (i // 2) * (1 - 2 * (i % 2))

    def taker(slot):
        return plane(near(slot // 4), near(slot % 4))

    def owner(slot):
        return plane(4 - near(slot // 4), 4 - near(slot % 4))

    def pillar(dz, other):
        to_z = lax.rem(z + dz, 8)
        to_core = 1 - core if other else core
        return (y * 4 + (to_z % 2) * 2 + to_core, x * 4 + to_z // 2)

    def remote(src, dst, send, recv, device):
        return pltpu.make_async_remote_copy(
            src_ref=src, dst_ref=dst, send_sem=send, recv_sem=recv, device_id=device, device_id_type=MESH
        )

    loads = [
        pltpu.make_async_copy(points_hbm, own.at[pl.ds(0, FEAT)], in_sem.at[0]),
        pltpu.make_async_copy(dir_hbm, own.at[pl.ds(FEAT, PROBES)], in_sem.at[1]),
        pltpu.make_async_copy(res_hbm, res, in_sem.at[2]),
    ]
    barrier = pltpu.get_barrier_semaphore()
    for s in reversed(range(1, GROUP)):
        pl.semaphore_signal(barrier, inc=1, device_id=pillar(*KEYS[s]), device_id_type=MESH)
        pl.semaphore_signal(barrier, inc=1, device_id=taker(s), device_id_type=MESH)
    for load in loads:
        load.start()
    for load in loads:
        load.wait()
    at_row = lax.broadcasted_iota(jnp.int32, (FEAT, FEAT), 0)
    at_lane = lax.broadcasted_iota(jnp.int32, (FEAT, FEAT), 1)
    factor = jnp.sum(jnp.where(at_row == at_lane, inverse_ref[...], 0.0), axis=1, keepdims=True)
    factor = factor * math.sqrt(math.log2(math.e))

    def prep_key(slot, source):
        rows = jnp.concatenate(features(source[0:FEAT], factor, True), axis=0)
        kf[slot * BLOCK:(slot + 1) * BLOCK, :] = rows.T
        vec = source[FEAT:FEAT + PROBES]
        high = vec.astype(BF16).astype(F32)
        db[:, slot * BLOCK:(slot + 1) * BLOCK] = jnp.concatenate([high, vec - high], axis=0).astype(BF16)
        wide = vec * DSCALE
        first = wide.astype(F8).astype(F32)
        d8[:, slot * BLOCK:(slot + 1) * BLOCK] = jnp.concatenate([first, wide - first], axis=0).astype(F8)

    def prep_query(slot, source):
        lanes = pl.ds(pl.multiple_of(slot * BLOCK, BLOCK), BLOCK)
        for i, part in enumerate(features(source, factor, False)):
            qf[i * FEAT:(i + 1) * FEAT, lanes] = part

    prep_key(0, own)
    prep_query(0, own[0:FEAT])
    pl.semaphore_wait(barrier, 2 * (GROUP - 1))

    q_copies, k_copies = {}, {}
    for s in (1, 2, 3, 6, 8, 10, 12):
        k_copies[s] = remote(own, kbuf.at[s], k_send.at[s], k_recv.at[s], pillar(*KEYS[s]))
    for s in range(1, GROUP):
        q_copies[s] = remote(
            own.at[pl.ds(0, FEAT)], qbuf.at[s], q_send.at[s], q_recv.at[s // 4], taker(s)
        )
    for s in range(1, GROUP):
        if s in k_copies:
            k_copies[s].start()
        q_copies[s].start()
    k_copies[FAR] = remote(kbuf.at[FAR - 2], kbuf.at[FAR], k_send.at[FAR], k_recv.at[FAR], pillar(7, 0))

    def forward(slot):
        to = RELAYED[slot]
        return remote(kbuf.at[slot], kbuf.at[to], f_send.at[slot], k_recv.at[to], pillar(0, 1))

    def relay(*slots):
        for slot in slots:
            k_copies[slot].wait_recv()
            forward(slot).start()
            if slot == FAR - 2:
                k_copies[FAR].start()

    def wait_keys(start, stop):
        for slot in range(start, stop):
            if slot == 1:
                k_copies[1].wait_recv()
            elif slot not in RELAYED:
                remote(own, kbuf.at[slot], k_send.at[slot], k_recv.at[slot], pillar(0, 1)).wait_recv()

    def prep_keys(start, stop):
        for slot in range(start, stop):
            prep_key(slot, kbuf.at[slot])

    def wait_queries(group, skip):
        blocks = qbuf.at[pl.ds(group * 4 + skip, 4 - skip)]
        remote(blocks, blocks, q_send.at[0], q_recv.at[group], taker(0)).wait_recv()

    def exponents(q, k, at):
        lanes = pl.ds(pl.multiple_of(q * QCHUNK, QCHUNK), QCHUNK)
        xs[at][...] = jnp.dot(kf[k * KCHUNK:(k + 1) * KCHUNK, :], qf[:, lanes], preferred_element_type=F32)

    def entries(at):
        value = jnp.exp2(jnp.minimum(xs[at][...], TOP))
        high = value.astype(BF16)
        hs[at][...] = high
        ls[at][...] = (value - high.astype(F32)).astype(F8)

    def products(k, at):
        keys = slice(k * KCHUNK, (k + 1) * KCHUNK)
        high = jnp.dot(db[:, keys], hs[at][...], preferred_element_type=F32)
        low = jnp.dot(d8[:, keys], ls[at][...], preferred_element_type=F32)
        return high + low * (1.0 / DSCALE)

    def block(first, second):
        exponents(*first, 0)
        exponents(*second, 1)
        entries(0)
        one = products(first[1], 0)
        entries(1)
        return one, products(second[1], 1)

    def give(slot, device):
        return remote(rs_out.at[slot], rs_in.at[slot], rs_send.at[slot], rs_recv.at[0], device)

    wait_keys(1, 2)
    relay(2, 3)
    wait_queries(0, 1)
    prep_keys(1, 4)
    for s in range(1, 2 * QPER):
        prep_query(s, qbuf[s])
    acc[0], acc[1] = block((0, 0), (1, 0))

    def first_keys(p, carry):
        wait_queries(p, 0)
        for i in range(2 * QPER):
            prep_query(p * 2 * QPER + i, qbuf[p * 2 * QPER + i])

        for at, slots in RELAYS_FIRST:
            pl.when(p == at)(functools.partial(relay, *slots))

        acc[2 * p], acc[2 * p + 1] = block((2 * p, 0), (2 * p + 1, 0))
        return carry

    lax.fori_loop(1, QCHUNKS // 2, first_keys, 0)
    wait_keys(4, 8)
    prep_keys(4, 8)

    def second_keys(p, carry):
        for at, slots in RELAYS_SECOND:
            pl.when(p == at)(functools.partial(relay, *slots))

        one, two = block((2 * p, 1), (2 * p + 1, 1))
        acc[2 * p] += one
        acc[2 * p + 1] += two
        return carry

    lax.fori_loop(0, QCHUNKS // 2, second_keys, 0)
    wait_keys(8, 16)
    prep_keys(8, 16)

    def last_keys(i, carry):
        q = QCHUNKS - 1 - i
        one, two = block((q, 2), (q, 3))
        total = acc[q] + one + two
        image = (total[0:PROBES] + total[PROBES:2 * PROBES]) * (2.0 ** -TOP)
        for j in range(QPER):
            rs_out[q * QPER + j] = image[:, j * BLOCK:(j + 1) * BLOCK]
        for j in range(QPER):
            slot = q * QPER + j

            @pl.when(slot > 0)
            def _():
                give(slot, owner(slot)).start()

        return carry

    lax.fori_loop(0, QCHUNKS, last_keys, 0)

    others = rs_in.at[pl.ds(1, GROUP - 1)]
    remote(others, others, rs_send.at[0], rs_recv.at[0], taker(0)).wait_recv()
    image = rs_out[0] + jnp.sum(rs_in[1:], axis=0)

    vec, resid = own[FEAT:FEAT + PROBES], res[...]
    image_ref[...] = image
    terms = [resid * resid, vec * image, resid * image, image * image]
    terms = jnp.concatenate([term[:, :128] + term[:, 128:] for term in terms] * 2, axis=0)
    sums = jnp.sum(terms.T, axis=0, keepdims=True)

    pair[0:1] = sums
    swap = remote(pair.at[pl.ds(0, 1)], pair.at[pl.ds(1, 1)], a1_send.at[0], a1_recv.at[0], pillar(0, 1))
    swap.start()
    swap.wait_recv()
    chips[0:1] = pair[0:1] + pair[1:2]
    for s in reversed(range(1, CHIPS)):
        dx, dy, dz = near(s // 32), near(s // 8 % 4), (s % 8 + 1) // 2 * (1 if s % 2 else 7)
        to_z = lax.rem(z + dz, 8)
        device = (lax.rem(y + dy, 4) * 4 + to_z % 2 * 2 + core, lax.rem(x + dx, 4) * 4 + to_z // 2)
        remote(chips.at[pl.ds(0, 1)], chips.at[pl.ds(s, 1)], a2_send.at[0], a2_recv.at[0], device).start()
    others = chips.at[pl.ds(1, CHIPS - 1)]
    everyone = remote(others, others, a2_send.at[0], a2_recv.at[0], pillar(0, 1))
    everyone.wait_recv()
    sums = jnp.sum(chips[...], axis=0, keepdims=True)

    columns = jnp.broadcast_to(sums, (BLOCK, 128)).T
    old_norm, curvature, cross, square = (columns[i * PROBES:(i + 1) * PROBES] for i in range(4))
    step = old_norm / curvature
    new_norm = old_norm - 2.0 * step * cross + step * step * square
    step_ref[...] = step
    ratio_ref[...] = new_norm / old_norm

    for s in range(1, GROUP):
        q_copies[s].wait_send()
        give(s, plane(0, 0)).wait_send()
    for slot, copy in k_copies.items():
        copy.wait_send()
    for slot in RELAYED:
        forward(slot).wait_send()
    swap.wait_send()
    everyone.wait_send()


def on_device(points, inv_length, solution_, residual, direction):
    vmem, hbm = pl.BlockSpec(memory_space=pltpu.VMEM), pl.BlockSpec(memory_space=pl.ANY)
    dma = pltpu.SemaphoreType.DMA
    image, step, ratio = pl.pallas_call(
        lambda *refs: cg_kernel(*refs[:15], refs[15:17], refs[17:19], refs[19:21], *refs[21:]),
        out_shape=(jax.ShapeDtypeStruct((PROBES, BLOCK), F32),) * 3,
        in_specs=[hbm, vmem, hbm, hbm],
        out_specs=(vmem, vmem, vmem),
        scratch_shapes=[
            pltpu.VMEM((FEAT + PROBES, BLOCK), F32),
            pltpu.VMEM((PROBES, BLOCK), F32),
            pltpu.VMEM((GROUP, FEAT + PROBES, BLOCK), F32),
            pltpu.VMEM((GROUP, FEAT, BLOCK), F32),
            pltpu.VMEM((GROUP * BLOCK, DEPTH), BF16),
            pltpu.VMEM((DEPTH, GROUP * BLOCK), BF16),
            pltpu.VMEM((2 * PROBES, GROUP * BLOCK), BF16),
            pltpu.VMEM((2 * PROBES, GROUP * BLOCK), F8),
        ]
        + [pltpu.VMEM((KCHUNK, QCHUNK), F32)] * 2
        + [pltpu.VMEM((KCHUNK, QCHUNK), BF16)] * 2
        + [pltpu.VMEM((KCHUNK, QCHUNK), F8)] * 2
        + [
            pltpu.VMEM((QCHUNKS, 2 * PROBES, QCHUNK), F32),
            pltpu.VMEM((GROUP, PROBES, BLOCK), F32),
            pltpu.VMEM((GROUP, PROBES, BLOCK), F32),
            pltpu.VMEM((8, 128), F32),
            pltpu.VMEM((CHIPS, 128), F32),
            dma((3,)),
        ]
        + [dma((GROUP,))] * 11,
        compiler_params=pltpu.CompilerParams(
            collective_id=0, has_side_effects=True, vmem_limit_bytes=VMEM_LIMIT
        ),
    )(points, inv_length[None, :], residual, direction)
    new_residual = residual - step * image
    return solution_ + step * direction, new_residual, new_residual + ratio * direction


def solution(mesh):
    split = P(None, ("row", "col"))
    return jax.shard_map(
        on_device,
        mesh=mesh,
        in_specs=(split, P(), split, split, split),
        out_specs=(split, split, split),
        check_vma=False,
    )
```

time: 56.8 us -> 52.6 us (0.926)
  Pallas kernels: 54.4 us -> 50.2 us
    pallas_call x1, Pallas kernels: 54.4 us -> 50.2 us  [on_device(): pl.pallas_call(lambda *refs: cg_kernel(*refs[:15], refs[15:17], refs[17:1...]
where the time goes in v3:
time: 52.6 us; the launch traced here: 52.2 us
  Pallas kernels  50.2 us (95%)
  other arithmetic  1.38 us (3%)
  between operations  0.69 us (1%)
    pallas_call x1, Pallas kernels, on_device(): pl.pallas_call(lambda *refs: cg_kernel(*refs[:15], refs[15:17], refs[17:1...  50.2 us
    add x1, other arithmetic, on_device(): new_residual + ratio * direction  1.38 us

profile of v3, /device:TPU:1, one launch (start us, length us, event | category | flops | bytes accessed | tf_op | source)
XLA Modules:
  0.0 52.2 jit_solution(249621133317353319)
XLA Ops:
  0.6 0.0 copy-start
  0.6 0.0 copy-start.1
  0.7 0.0 copy-start.2
  0.7 50.2 %shard_map.76 = (f32[16,256]{1,0:T(8,128)}, f32[16,256]{1,0:T(8,128)}, f32[16,256]{1,0:T(8,128)}) custom-call(f32[16,256]{1,0:T(8,128)} %refs_0_.1, f32[1,16]{1,0:T(1,128)} %bitcast.1, f32[16,256]{1,0:T(8,128)} %refs_2_.1, f32[16,256]{1,0:T(8,128)} %refs_3_.1), custom_call_target="tpu_custom_call" | custom-call | tf_op jit(solution)/shard_map/pallas_call | solution.py:299
  50.8 0.0 copy-done
  50.8 0.0 copy-done.1
  50.9 0.0 copy-done.2
  50.9 1.4 %multiply_add_fusion = (f32[16,256]{1,0:T(8,128)}, f32[16,256]{1,0:T(8,128)}, f32[16,256]{1,0:T(8,128)}) fusion(f32[16,256]{1,0:T(8,128)} %get-tuple-element.8, f32[16,256]{1,0:T(8,128)S(1)} %copy-done.1, f32[16,256]{1,0:T(8,128)S(1)} %copy-done, f32[16,256]{1,0:T(8,128)} %get-tuple-element.6, f32[16,256]{1,0:T(8,128)} %get-tuple-element.7, ...), kind=kLoop, calls=%fused_computation | loop fusion | flops 24576 | bytes 147456 | tf_op jit(solution)/shard_map/add | solution.py:331
Async XLA Ops:
  0.6 50.2 %copy-start = (f32[16,256]{1,0:T(8,128)S(1)}, f32[16,256]{1,0:T(8,128)}, u32[]{:S(2)}) copy-start(f32[16,256]{1,0:T(8,128)} %refs_2_.1) | copy-start | bytes 49156
  0.6 50.2 %copy-start.1 = (f32[16,256]{1,0:T(8,128)S(1)}, f32[16,256]{1,0:T(8,128)}, u32[]{:S(2)}) copy-start(f32[16,256]{1,0:T(8,128)} %refs_3_.1) | copy-start | bytes 49156
  0.7 50.2 %copy-start.2 = (f32[16,256]{1,0:T(8,128)S(1)}, f32[16,256]{1,0:T(8,128)}, u32[]{:S(2)}) copy-start(f32[16,256]{1,0:T(8,128)} %param.7) | copy-start | bytes 49156

commit v4 on v3

--- a/solution.py
+++ b/solution.py
@@ -25,12 +25,17 @@
 QCHUNK = QPER * BLOCK
 QCHUNKS = GROUP // QPER
 VMEM_LIMIT = 60 * 2**20
-RELAYS_FIRST = ((2, (6,)), (3, (12,)))
-RELAYS_SECOND = ((0, (8, 10)), (2, (14,)))
+RELAYS = ((6,), (12,), (8, 10), (), (14,), ())
 DEPTH = 128
 TOP = 17.0
 DSCALE = 32.0
 KEYS = ((0, 0), (0, 1), (1, 0), (7, 0), (1, 1), (7, 1), (2, 0), (2, 1), (6, 0), (6, 1), (3, 0), (3, 1), (5, 0), (5, 1), (4, 0), (4, 1))
+PLANE = (
+    (0, 0), (0, 1), (0, 3), (1, 0), (3, 0), (1, 1), (1, 3), (3, 1),
+    (3, 3), (0, 2), (2, 0), (1, 2), (3, 2), (2, 1), (2, 3), (2, 2),
+)
+NEAR_PLANE = tuple(range(1, 11))
+NEAR_KEYS = (1, 2, 3, 6, 8)
 FAR = KEYS.index((4, 0))
 RELAYED = {KEYS.index((dz, 0)): KEYS.index((dz, 1)) for dz in range(1, 8)}
 
@@ -78,10 +83,10 @@
         return i + (i // 2) * (1 - 2 * (i % 2))
 
     def taker(slot):
-        return plane(near(slot // 4), near(slot % 4))
+        return plane(*PLANE[slot])
 
     def owner(slot):
-        return plane(4 - near(slot // 4), 4 - near(slot % 4))
+        return plane(4 - PLANE[slot][0], 4 - PLANE[slot][1])
 
     def pillar(dz, other):
         to_z = lax.rem(z + dz, 8)
@@ -99,12 +104,13 @@
         pltpu.make_async_copy(res_hbm, res, in_sem.at[2]),
     ]
     barrier = pltpu.get_barrier_semaphore()
-    for s in reversed(range(1, GROUP)):
+    for s in reversed(NEAR_PLANE):
+        pl.semaphore_signal(barrier, inc=1, device_id=taker(s), device_id_type=MESH)
+    for s in reversed(NEAR_KEYS):
         pl.semaphore_signal(barrier, inc=1, device_id=pillar(*KEYS[s]), device_id_type=MESH)
-        pl.semaphore_signal(barrier, inc=1, device_id=taker(s), device_id_type=MESH)
     for load in loads:
         load.start()
-    for load in loads:
+    for load in loads[:2]:
         load.wait()
     at_row = lax.broadcasted_iota(jnp.int32, (FEAT, FEAT), 0)
     at_lane = lax.broadcasted_iota(jnp.int32, (FEAT, FEAT), 1)
@@ -128,7 +134,7 @@
 
     prep_key(0, own)
     prep_query(0, own[0:FEAT])
-    pl.semaphore_wait(barrier, 2 * (GROUP - 1))
+    pl.semaphore_wait(barrier, len(NEAR_PLANE) + len(NEAR_KEYS))
 
     q_copies, k_copies = {}, {}
     for s in (1, 2, 3, 6, 8, 10, 12):
@@ -137,8 +143,8 @@
         q_copies[s] = remote(
             own.at[pl.ds(0, FEAT)], qbuf.at[s], q_send.at[s], q_recv.at[s // 4], taker(s)
         )
-    for s in range(1, GROUP):
-        if s in k_copies:
+    for s in NEAR_PLANE:
+        if s in NEAR_KEYS:
             k_copies[s].start()
         q_copies[s].start()
     k_copies[FAR] = remote(kbuf.at[FAR - 2], kbuf.at[FAR], k_send.at[FAR], k_recv.at[FAR], pillar(7, 0))
@@ -199,28 +205,33 @@
     wait_keys(1, 2)
     relay(2, 3)
     wait_queries(0, 1)
+    for s in (10, 12):
+        k_copies[s].start()
+    for s in range(11, 15):
+        q_copies[s].start()
     prep_keys(1, 4)
     for s in range(1, 2 * QPER):
         prep_query(s, qbuf[s])
     acc[0], acc[1] = block((0, 0), (1, 0))
 
-    def first_keys(p, carry):
+    def take_queries(p):
         wait_queries(p, 0)
         for i in range(2 * QPER):
             prep_query(p * 2 * QPER + i, qbuf[p * 2 * QPER + i])
 
-        for at, slots in RELAYS_FIRST:
-            pl.when(p == at)(functools.partial(relay, *slots))
-
-        acc[2 * p], acc[2 * p + 1] = block((2 * p, 0), (2 * p + 1, 0))
-        return carry
-
-    lax.fori_loop(1, QCHUNKS // 2, first_keys, 0)
+    wait_queries(1, 0)
+    q_copies[15].start()
+    for i in range(2 * QPER, 4 * QPER):
+        prep_query(i, qbuf[i])
+    acc[2], acc[3] = block((2, 0), (3, 0))
+    take_queries(2)
+    relay(*RELAYS[0])
+    acc[4], acc[5] = block((4, 0), (5, 0))
     wait_keys(4, 8)
     prep_keys(4, 8)
 
     def second_keys(p, carry):
-        for at, slots in RELAYS_SECOND:
+        for at, slots in enumerate(RELAYS[1:4]):
             pl.when(p == at)(functools.partial(relay, *slots))
 
         one, two = block((2 * p, 1), (2 * p + 1, 1))
@@ -228,7 +239,13 @@
         acc[2 * p + 1] += two
         return carry
 
-    lax.fori_loop(0, QCHUNKS // 2, second_keys, 0)
+    lax.fori_loop(0, QCHUNKS // 2 - 1, second_keys, 0)
+    take_queries(3)
+    relay(*RELAYS[4])
+    for q in (6, 7):
+        one, two = block((q, 0), (q, 1))
+        acc[q] = one + two
+    relay(*RELAYS[5])
     wait_keys(8, 16)
     prep_keys(8, 16)
 
@@ -239,12 +256,12 @@
         image = (total[0:PROBES] + total[PROBES:2 * PROBES]) * (2.0 ** -TOP)
         for j in range(QPER):
             rs_out[q * QPER + j] = image[:, j * BLOCK:(j + 1) * BLOCK]
-        for j in range(QPER):
-            slot = q * QPER + j
-
-            @pl.when(slot > 0)
+        for chunk in range(QCHUNKS):
+
+            @pl.when(q == chunk)
             def _():
-                give(slot, owner(slot)).start()
+                for slot in range(max(1, chunk * QPER), (chunk + 1) * QPER):
+                    give(slot, owner(slot)).start()
 
         return carry
 
@@ -254,6 +271,7 @@
     remote(others, others, rs_send.at[0], rs_recv.at[0], taker(0)).wait_recv()
     image = rs_out[0] + jnp.sum(rs_in[1:], axis=0)
 
+    loads[2].wait()
     vec, resid = own[FEAT:FEAT + PROBES], res[...]
     image_ref[...] = image
     terms = [resid * resid, vec * image, resid * image, image * image]
@@ -298,7 +316,7 @@
     dma = pltpu.SemaphoreType.DMA
     image, step, ratio = pl.pallas_call(
         lambda *refs: cg_kernel(*refs[:15], refs[15:17], refs[17:19], refs[19:21], *refs[21:]),
-        out_shape=(jax.ShapeDtypeStruct((PROBES, BLOCK), F32),) * 3,
+        out_shape=(pltpu.VMEM((PROBES, BLOCK), F32),) * 3,
         in_specs=[hbm, vmem, hbm, hbm],
         out_specs=(vmem, vmem, vmem),
         scratch_shapes=[

time: 52.6 us -> 50.4 us (0.958)
  Pallas kernels: 50.2 us -> 48.9 us
  other arithmetic: 1.38 us -> 0.63 us
    pallas_call x1, Pallas kernels: 50.2 us -> 48.9 us  [on_device(): pl.pallas_call(lambda *refs: cg_kernel(*refs[:15], refs[15:17], refs[17:1...]
    add x1, other arithmetic: 1.38 us -> 0.63 us  [on_device(): new_residual + ratio * direction]
where the time goes in v4:
time: 50.4 us; the launch traced here: 50.3 us
  Pallas kernels  48.9 us (97%)
  between operations  0.69 us (1%)
  other arithmetic  0.63 us (1%)
    pallas_call x1, Pallas kernels, on_device(): pl.pallas_call(lambda *refs: cg_kernel(*refs[:15], refs[15:17], refs[17:1...  48.9 us

profile of v4, /device:TPU:1, one launch (start us, length us, event | category | flops | bytes accessed | tf_op | source)
XLA Modules:
  0.0 50.3 jit_solution(4734765916853508466)
XLA Ops:
  0.6 0.0 copy-start
  0.6 0.0 copy-start.1
  0.7 0.0 copy-start.2
  0.7 48.9 %shard_map.76 = (f32[16,256]{1,0:T(8,128)S(1)}, f32[16,256]{1,0:T(8,128)S(1)}, f32[16,256]{1,0:T(8,128)S(1)}) custom-call(f32[16,256]{1,0:T(8,128)} %refs_0_.1, f32[1,16]{1,0:T(1,128)} %bitcast.1, f32[16,256]{1,0:T(8,128)} %refs_2_.1, f32[16,256]{1,0:T(8,128)} %refs_3_.1), custom_call_target="tpu_custom_call" | custom-call | tf_op jit(solution)/shard_map/pallas_call | solution.py:317
  49.6 0.0 copy-done
  49.6 0.0 copy-done.1
  49.6 0.0 copy-done.2
  49.6 0.6 %multiply_add_fusion = (f32[16,256]{1,0:T(8,128)}, f32[16,256]{1,0:T(8,128)}, f32[16,256]{1,0:T(8,128)}) fusion(f32[16,256]{1,0:T(8,128)S(1)} %get-tuple-element.8, f32[16,256]{1,0:T(8,128)S(1)} %copy-done.1, f32[16,256]{1,0:T(8,128)S(1)} %copy-done, f32[16,256]{1,0:T(8,128)S(1)} %get-tuple-element.6, f32[16,256]{1,0:T(8,128)S(1)} %get-tuple-element.7, ...), kind=kLoop, calls=%fused_computation | loop fusion | flops 24576 | bytes 147456 | tf_op jit(solution)/shard_map/add | solution.py:349
Async XLA Ops:
  0.6 49.0 %copy-start = (f32[16,256]{1,0:T(8,128)S(1)}, f32[16,256]{1,0:T(8,128)}, u32[]{:S(2)}) copy-start(f32[16,256]{1,0:T(8,128)} %refs_2_.1) | copy-start | bytes 49156
  0.6 49.0 %copy-start.1 = (f32[16,256]{1,0:T(8,128)S(1)}, f32[16,256]{1,0:T(8,128)}, u32[]{:S(2)}) copy-start(f32[16,256]{1,0:T(8,128)} %refs_3_.1) | copy-start | bytes 49156
  0.7 49.0 %copy-start.2 = (f32[16,256]{1,0:T(8,128)S(1)}, f32[16,256]{1,0:T(8,128)}, u32[]{:S(2)}) copy-start(f32[16,256]{1,0:T(8,128)} %param.7) | copy-start | bytes 49156
